TPU v7x, 32 devices: a whole 2x2x4 slice. The times are simulated.
32 devices in a mesh: seq: 4 (over x, core), head: 8 (over z, y).
Axes of the slice: x: 2, y: 2, z: 4, core: 2. Of those that a mesh axis runs over, the one named last changes fastest.
Arguments:
- queries: bfloat16 [4096, 2560], P('seq', 'head'), may hold values from -6 to 6
- key_vectors: bfloat16 [4096, 2560], P('seq', 'head'), may hold values from -6 to 6
- value_vectors: bfloat16 [4096, 2560], P('seq', 'head'), may hold values from -6 to 6
- fast_gate: float32 [8, 320, 320], P('head'), may hold values from -0.3125 to 0.3125
- fast_up: float32 [8, 320, 320], P('head'), may hold values from -0.3125 to 0.3125
- fast_down: float32 [8, 320, 320], P('head'), may hold values from -1 to 1
- step_sizes: float32 [8], P('head'), may hold values from 0.2 to 1
- out_gain: float32 [2560], P('head'), may hold values from 0.25 to 1.75
Outputs:
- layer_output: float32 [4, 1024, 2560], P(None, 'seq', 'head')
All inputs are finite; a program needn't handle non-finite values.
Results may differ from a plain program's by a relative error of at most 0.038.
Values may be sent and summed in bfloat16 or wider, within the bound.
A program may use at most 64 MiB of HBM per device.

v0:
```python
import functools
import math

import jax
import jax.numpy as jnp
from jax import lax
from jax.experimental import pallas as pl
from jax.experimental.pallas import tpu as pltpu
from jax.sharding import PartitionSpec as P

GROUPS = 2
NS_ITERS = 4
LANES = 128

newton_coefs = (3.4445, -4.775, 2.0315)
MESH = pl.DeviceIdType.MESH
BF = jnp.bfloat16
F32 = jnp.float32


def dot(left, right, left_dim, right_dim):
    return lax.dot_general(
        left, right, (((left_dim,), (right_dim,)), ((), ())), preferred_element_type=F32
    )


def rms_rows(rows):
    rows = rows.astype(F32)
    return (rows * lax.rsqrt(jnp.mean(rows * rows, -1, keepdims=True) + 1e-06)).astype(BF)


def kernel(
    seq_count,
    head_count,
    q_ref,
    k_ref,
    v_ref,
    gate_ref,
    up_ref,
    down_ref,
    step_ref,
    gain_ref,
    out_ref,
    q_all,
    att_own,
    att_all,
    tail_k,
    tail_v,
    key_t,
    val_t,
    grad_f,
    grad_b,
    grad_in,
    sums,
    weights,
    fast,
    squares,
    send_q,
    recv_q,
    send_att,
    recv_att,
    send_tail,
    recv_tail,
    send_part,
    recv_part,
    send_sum,
    recv_sum,
    send_cross,
    send_sq,
    recv_sq,
):
    rows, dh = q_ref.shape
    window = rows // 2
    members = seq_count // GROUPS
    out_rows = rows // seq_count
    group_rows = rows // GROUPS
    chunk = grad_in.shape[1]
    width = dh * head_count
    me = lax.axis_index("seq")
    head = lax.axis_index("head")
    own_group = me // members
    own_member = lax.rem(me, members)

    def remote(src, dst, send, recv, seq, hd):
        return pltpu.make_async_remote_copy(
            src_ref=src,
            dst_ref=dst,
            send_sem=send,
            recv_sem=recv,
            device_id=(seq, hd),
            device_id_type=MESH,
        )

    def rows_of(index, size):
        return pl.ds(pl.multiple_of(index * size, size), size)

    barrier = pltpu.get_barrier_semaphore()
    for d in range(1, seq_count):
        pl.semaphore_signal(
            barrier, inc=1, device_id=(lax.rem(me + d, seq_count), head), device_id_type=MESH
        )
    for d in range(1, head_count):
        pl.semaphore_signal(
            barrier, inc=1, device_id=(me, lax.rem(head + d, head_count)), device_id_type=MESH
        )

    key_t[...] = jnp.transpose(rms_rows(k_ref[...]).astype(F32)).astype(BF)
    val_t[...] = jnp.transpose(-v_ref[...].astype(F32)).astype(BF)
    weights[0] = gate_ref[0]
    weights[1] = up_ref[0]
    weights[2] = down_ref[0]
    q_all[me] = q_ref[rows_of(me, out_rows), :]
    spare = members * chunk - 3 * dh
    if spare:
        grad_f[3 * dh :, :] = jnp.zeros((spare, dh), F32)
        grad_b[3 * dh :, :] = jnp.zeros((spare, dh), BF)

    @pl.when(me == 0)
    def _():
        tail_k[...] = jnp.zeros(tail_k.shape, BF)
        tail_v[...] = jnp.zeros(tail_v.shape, BF)

    pl.semaphore_wait(barrier, seq_count + head_count - 2)

    def q_copy(d, slot):
        return remote(
            q_ref.at[pl.ds(d * out_rows, out_rows), :],
            q_all.at[slot],
            send_q.at[d],
            recv_q.at[slot],
            d,
            head,
        )

    def tail_copy(which, target):
        source = (k_ref, v_ref)[which]
        landing = (tail_k, tail_v)[which]
        return remote(
            source.at[pl.ds(rows - window, window), :],
            landing,
            send_tail.at[which],
            recv_tail.at[which],
            target,
            head,
        )

    def send_inputs():
        @pl.when(me < seq_count - 1)
        def _():
            tail_copy(0, me + 1).start()
            tail_copy(1, me + 1).start()

        for d in range(seq_count):

            @pl.when(me != d)
            def _():
                q_copy(d, me).start()

    scale = 1.0 / math.sqrt(dh)
    block = min(256, window)

    def attend(start):
        queries = q_ref[start : start + block, :]
        if start < window:
            keys = jnp.concatenate([tail_k[start:, :], k_ref[: start + block, :]], 0)
            values = jnp.concatenate([tail_v[start:, :], v_ref[: start + block, :]], 0)
        else:
            keys = k_ref[start - window : start + block, :]
            values = v_ref[start - window : start + block, :]
        scores = dot(queries, keys, 1, 1) * scale
        row = lax.broadcasted_iota(jnp.int32, scores.shape, 0)
        col = lax.broadcasted_iota(jnp.int32, scores.shape, 1)
        allowed = (col <= row + window) & (col > row)
        if start < window:
            allowed = allowed & (col >= jnp.where(me == 0, window - start, 0))
        scores = jnp.where(allowed, scores, -1e30)
        highest = jnp.max(scores, -1, keepdims=True)
        expo = jnp.where(allowed, jnp.exp(scores - highest), 0.0)
        probs = (expo / jnp.sum(expo, -1, keepdims=True)).astype(BF)
        att_own[start : start + block, :] = dot(probs, values, 1, 0).astype(BF)

    def att_copy(d, slot):
        return remote(
            att_own.at[pl.ds(d * out_rows, out_rows), :],
            att_all.at[slot],
            send_att.at[d],
            recv_att.at[slot],
            d,
            head,
        )

    def attend_half(first):
        begin = 0 if first else window
        if first:

            @pl.when(me > 0)
            def _():
                tail_copy(0, me).wait_recv()
                tail_copy(1, me).wait_recv()

        for start in range(begin, begin + window, block):
            attend(start)
        for d in range(begin // out_rows, (begin + window) // out_rows):

            @pl.when(me != d)
            def _():
                att_copy(d, me).start()

            @pl.when(me == d)
            def _():
                att_all[d] = att_own[d * out_rows : (d + 1) * out_rows, :]

    token_block = min(256, rows)

    def gradients():
        wb = [weights[i].astype(BF) for i in range(3)]
        totals = [None] * 3
        for start in range(0, rows, token_block):
            keys = key_t[:, start : start + token_block]
            values = val_t[:, start : start + token_block]
            gate = dot(wb[0], keys, 0, 0)
            upward = dot(wb[1], keys, 0, 0)
            back = dot(wb[2], values, 1, 0)
            sigma = jax.nn.sigmoid(gate)
            active = gate * sigma
            hidden = (active * upward).astype(BF)
            slope = sigma * (1.0 + gate * (1.0 - sigma))
            grad_gate = (back * upward * slope).astype(BF)
            grad_up = (back * active).astype(BF)
            parts = [
                dot(keys, grad_gate, 1, 1),
                dot(keys, grad_up, 1, 1),
                dot(hidden, values, 1, 1),
            ]
            totals = [p if t is None else t + p for t, p in zip(totals, parts)]
        for i in range(3):
            grad_f[i * dh : (i + 1) * dh, :] = totals[i]
            grad_b[i * dh : (i + 1) * dh, :] = totals[i].astype(BF)

    def part_copy(group, target, slot):
        return remote(
            grad_b.at[pl.ds(target * chunk, chunk), :],
            grad_in.at[slot],
            send_part.at[target],
            recv_part.at[slot],
            group * members + target,
            head,
        )

    def sum_copy(group, piece, send, seq):
        place = sums.at[group, rows_of(piece, chunk), :]
        return remote(place, place, send, recv_sum.at[group, piece], seq, head)

    def spread(group):
        for m in range(members):

            @pl.when(own_member != m)
            def _():
                sum_copy(
                    group, own_member, send_sum.at[group, m], own_group * members + m
                ).start()

    def group_sums(group):
        gradients()
        for m in range(members):

            @pl.when(own_member != m)
            def _():
                part_copy(group, m, own_member).start()

        place = rows_of(own_member, chunk)
        grad_in[own_member] = jnp.zeros(grad_in.shape[1:], BF)
        for m in range(members):

            @pl.when(own_member != m)
            def _():
                part_copy(group, m, m).wait_recv()

        total = grad_f[place, :]
        for m in range(members):
            total = total + grad_in[m].astype(F32)
        sums[group, place, :] = total.astype(BF)
        for other in range(GROUPS):
            if other != group:
                sum_copy(
                    group, own_member, send_cross.at[other], other * members + own_member
                ).start()
        spread(group)

    def collect_sums(group):
        @pl.when(own_group != group)
        def _():
            sum_copy(group, own_member, send_cross.at[group], me).wait_recv()
            spread(group)

        for m in range(members):

            @pl.when(own_member != m)
            def _():
                sum_copy(group, m, send_cross.at[group], me).wait_recv()

    def update(group):
        first, second, third = newton_coefs
        current = []
        for i in range(3):
            grads = sums[group, i * dh : (i + 1) * dh, :].astype(F32)
            total = jnp.sum(jnp.sum(grads * grads, 1, keepdims=True), 0, keepdims=True)
            current.append(grads * lax.rsqrt(total + 1e-06))
        for repeat in range(NS_ITERS):
            low = [x.astype(BF) for x in current]
            gram = [dot(x, x, 1, 1) for x in low]
            gram_low = [a.astype(BF) for a in gram]
            square = [dot(a, a, 1, 0) for a in gram_low]
            mixing = [(second * a + third * s).astype(BF) for a, s in zip(gram, square)]
            current = [
                first * x + dot(b, y, 1, 0) for x, b, y in zip(current, mixing, low)
            ]
        for i in range(3):
            weights[i] = weights[i] - step_ref[0] * current[i]

    def sq_copy(group, target, slot):
        return remote(
            squares.at[group, head],
            squares.at[group, slot],
            send_sq.at[group, target],
            recv_sq.at[group, slot],
            me,
            target,
        )

    def apply_group(group):
        for a in range(group * members, (group + 1) * members):

            @pl.when(me != a)
            def _():
                q_copy(0, a).wait_recv()

        wb = [weights[i].astype(BF) for i in range(3)]
        normed = rms_rows(
            q_all[group * members : (group + 1) * members].reshape(group_rows, dh)
        )
        gate = dot(normed, wb[0], 1, 0)
        upward = dot(normed, wb[1], 1, 0)
        hidden = (gate * jax.nn.sigmoid(gate) * upward).astype(BF)
        result = dot(hidden, wb[2], 1, 0)
        fast[group] = result
        line = dot(jnp.ones((8, dh), BF), (result * result).astype(BF), 1, 1)
        squares[group, head] = jnp.zeros(squares.shape[2:], F32)
        for i in range(group_rows // LANES):
            squares[group, head, i : i + 1, :] = line[0:1, i * LANES : (i + 1) * LANES]
        for h in range(head_count):

            @pl.when(head != h)
            def _():
                sq_copy(group, h, head).start()

    def finish_group(group):
        for a in range(group * members, (group + 1) * members):

            @pl.when(me != a)
            def _():
                att_copy(0, a).wait_recv()

        for h in range(head_count):

            @pl.when(head != h)
            def _():
                sq_copy(group, h, h).wait_recv()

        total = squares[group, 0]
        for h in range(1, head_count):
            total = total + squares[group, h]
        factor = jnp.transpose(lax.rsqrt(total / width + 1e-06))
        gain = gain_ref[...]
        piece = min(LANES, out_rows)
        for start in range(0, group_rows, piece):
            a, begin = group * members + start // out_rows, start % out_rows
            lane, low = start // LANES, start % LANES
            out_ref[a, begin : begin + piece, :] = (
                att_all[a, begin : begin + piece, :].astype(F32)
                + gain
                * fast[group, start : start + piece, :]
                * factor[low : low + piece, lane : lane + 1]
            )

    for group in range(GROUPS):

        @pl.when(own_group == group)
        def _():
            group_sums(group)
            if group == 0:
                send_inputs()
            else:
                attend_half(True)

        if group == 0:

            @pl.when(own_group != 0)
            def _():
                send_inputs()
                attend_half(False)

        else:
            if group == 1:

                @pl.when(own_group == 0)
                def _():
                    attend_half(False)
                    attend_half(True)

            apply_group(group - 1)
        collect_sums(group)
        update(group)
    apply_group(GROUPS - 1)
    for group in range(GROUPS):
        finish_group(group)

    @pl.when(me < seq_count - 1)
    def _():
        tail_copy(0, me + 1).wait_send()
        tail_copy(1, me + 1).wait_send()

    for d in range(seq_count):

        @pl.when(me != d)
        def _():
            q_copy(d, me).wait_send()
            att_copy(d, me).wait_send()

    for m in range(members):

        @pl.when(own_member != m)
        def _():
            part_copy(own_group, m, own_member).wait_send()
            for group in range(GROUPS):
                sum_copy(
                    group, own_member, send_sum.at[group, m], own_group * members + m
                ).wait_send()

    for other in range(GROUPS):

        @pl.when(own_group != other)
        def _():
            sum_copy(
                own_group, own_member, send_cross.at[other], other * members + own_member
            ).wait_send()

    for group in range(GROUPS):
        for h in range(head_count):

            @pl.when(head != h)
            def _():
                sq_copy(group, h, head).wait_send()


def solution(mesh):
    seq_count, head_count = mesh.shape["seq"], mesh.shape["head"]

    def on_device(
        queries, key_vectors, value_vectors, fast_gate, fast_up, fast_down, step_sizes, out_gain
    ):
        rows, dh = queries.shape
        window = rows // 2
        members = seq_count // GROUPS
        out_rows = rows // seq_count
        group_rows = rows // GROUPS
        chunk = -(-3 * dh // (members * 16)) * 16
        lines = max(8, group_rows // LANES)
        dma = pltpu.SemaphoreType.DMA
        vmem = pl.BlockSpec(memory_space=pltpu.VMEM)
        smem = pl.BlockSpec(memory_space=pltpu.SMEM)
        return pl.pallas_call(
            functools.partial(kernel, seq_count, head_count),
            out_shape=jax.ShapeDtypeStruct((seq_count, out_rows, dh), F32),
            in_specs=[vmem] * 6 + [smem, vmem],
            out_specs=vmem,
            scratch_shapes=[
                pltpu.VMEM((seq_count, out_rows, dh), BF),
                pltpu.VMEM((rows, dh), BF),
                pltpu.VMEM((seq_count, out_rows, dh), BF),
                pltpu.VMEM((window, dh), BF),
                pltpu.VMEM((window, dh), BF),
                pltpu.VMEM((dh, rows), BF),
                pltpu.VMEM((dh, rows), BF),
                pltpu.VMEM((members * chunk, dh), F32),
                pltpu.VMEM((members * chunk, dh), BF),
                pltpu.VMEM((members, chunk, dh), BF),
                pltpu.VMEM((GROUPS, members * chunk, dh), BF),
                pltpu.VMEM((3, dh, dh), F32),
                pltpu.VMEM((GROUPS, group_rows, dh), F32),
                pltpu.VMEM((GROUPS, head_count, lines, LANES), F32),
                dma((seq_count,)),
                dma((seq_count,)),
                dma((seq_count,)),
                dma((seq_count,)),
                dma((2,)),
                dma((2,)),
                dma((members,)),
                dma((members,)),
                dma((GROUPS, members)),
                dma((GROUPS, members)),
                dma((GROUPS,)),
                dma((GROUPS, head_count)),
                dma((GROUPS, head_count)),
            ],
            compiler_params=pltpu.CompilerParams(
                collective_id=0, has_side_effects=True, vmem_limit_bytes=48 * 1024 * 1024
            ),
        )(
            queries,
            key_vectors,
            value_vectors,
            fast_gate,
            fast_up,
            fast_down,
            step_sizes,
            out_gain.reshape(1, dh),
        )

    in_specs = (
        P("seq", "head"),
        P("seq", "head"),
        P("seq", "head"),
        P("head", None, None),
        P("head", None, None),
        P("head", None, None),
        P("head"),
        P("head"),
    )
    return jax.shard_map(
        on_device, mesh=mesh, in_specs=in_specs, out_specs=P(None, "seq", "head"), check_vma=False
    )
```

profile of v0, /device:TPU:1, one launch (start us, length us, event | category | flops | bytes accessed | tf_op | source)
XLA Modules:
  0.0 64.7 jit_solution(17891208309585745591)
XLA Ops:
  0.0 0.0 copy-start.5
  0.0 0.0 copy-start.4
  0.8 0.7 %reshape.3.gain_ref = f32[1,320]{1,0:T(1,128)S(1)} reshape(f32[320]{0:T(512)} %param.15) | data formatting | bytes 2560 | tf_op jit(solution)/shard_map/reshape | solution.py:517
  1.4 1.4 %copy.9.q_ref = bf16[1024,320]{1,0:T(8,128)(2,1)S(1)} copy(bf16[1024,320]{0,1:T(8,128)(2,1)} %param.8) | data formatting | bytes 1310720 | tf_op args[0]
  2.9 0.0 copy-done.4
  2.9 0.4 copy.10.k_ref
  3.3 0.0 copy-done.5
  3.3 1.2 %copy.11.v_ref = bf16[1024,320]{1,0:T(8,128)(2,1)} copy(bf16[1024,320]{0,1:T(8,128)(2,1)S(1)} %copy-done.5) | data formatting | bytes 1310720 | tf_op args[2]
  4.4 0.0 copy-start
  4.4 1.1 %copy-done = bf16[1024,320]{1,0:T(8,128)(2,1)S(1)} copy-done((bf16[1024,320]{1,0:T(8,128)(2,1)S(1)}, bf16[1024,320]{1,0:T(8,128)(2,1)}, u32[]{:S(2)}) %copy-start) | copy-done | bytes 655384
  5.6 0.0 copy-start.1
  5.6 1.0 %copy-done.1 = f32[1,320,320]{2,1,0:T(8,128)S(1)} copy-done((f32[1,320,320]{2,1,0:T(8,128)S(1)}, f32[1,320,320]{2,1,0:T(8,128)}, u32[]{:S(2)}) %copy-start.1) | copy-done | bytes 409624
  6.6 0.0 copy-start.2
  6.6 1.0 %copy-done.2 = f32[1,320,320]{2,1,0:T(8,128)S(1)} copy-done((f32[1,320,320]{2,1,0:T(8,128)S(1)}, f32[1,320,320]{2,1,0:T(8,128)}, u32[]{:S(2)}) %copy-start.2) | copy-done | bytes 409624
  7.6 0.0 copy-start.3
  7.6 1.0 %copy-done.3 = f32[1,320,320]{2,1,0:T(8,128)S(1)} copy-done((f32[1,320,320]{2,1,0:T(8,128)S(1)}, f32[1,320,320]{2,1,0:T(8,128)}, u32[]{:S(2)}) %copy-start.3) | copy-done | bytes 409624
  8.7 54.5 %shard_map.82 = f32[4,256,320]{2,1,0:T(8,128)S(1)} custom-call(bf16[1024,320]{1,0:T(8,128)(2,1)S(1)} %copy.9.q_ref, bf16[1024,320]{1,0:T(8,128)(2,1)S(1)} %copy.10.k_ref, bf16[1024,320]{1,0:T(8,128)(2,1)S(1)} %copy-done, f32[1,320,320]{2,1,0:T(8,128)S(1)} %copy-done.1, f32[1,320,320]{2,1,0:T(8,128)S(1)} %copy-done.2, f32[1,320,320]{2,1,0:T(8,128)S(1)} %copy-done.3, ...), custom_call_target="tpu_custom_call" | custom-call | tf_op jit(solution)/shard_map/pallas_call | solution.py:472
  63.2 1.5 %copy.12 = f32[4,256,320]{1,2,0:T(8,128)} copy(f32[4,256,320]{2,1,0:T(8,128)S(1)} %shard_map.82) | data formatting | bytes 2621440 | tf_op jit(solution)/shard_map/pallas_call | solution.py:472
Async XLA Ops:
  0.0 3.3 %copy-start.5 = (bf16[1024,320]{0,1:T(8,128)(2,1)S(1)}, bf16[1024,320]{0,1:T(8,128)(2,1)}, u32[]{:S(2)}) copy-start(bf16[1024,320]{0,1:T(8,128)(2,1)} %param.10) | copy-start | bytes 1966084
  0.0 2.9 %copy-start.4 = (bf16[1024,320]{0,1:T(8,128)(2,1)S(1)}, bf16[1024,320]{0,1:T(8,128)(2,1)}, u32[]{:S(2)}) copy-start(bf16[1024,320]{0,1:T(8,128)(2,1)} %param.9) | copy-start | bytes 1966084
  4.4 1.1 %copy-start = (bf16[1024,320]{1,0:T(8,128)(2,1)S(1)}, bf16[1024,320]{1,0:T(8,128)(2,1)}, u32[]{:S(2)}) copy-start(bf16[1024,320]{1,0:T(8,128)(2,1)} %copy.11.v_ref) | copy-start | bytes 1966084
  5.6 1.0 %copy-start.1 = (f32[1,320,320]{2,1,0:T(8,128)S(1)}, f32[1,320,320]{2,1,0:T(8,128)}, u32[]{:S(2)}) copy-start(f32[1,320,320]{2,1,0:T(8,128)} %gate_ref.1) | copy-start | bytes 1228804
  6.6 1.0 %copy-start.2 = (f32[1,320,320]{2,1,0:T(8,128)S(1)}, f32[1,320,320]{2,1,0:T(8,128)}, u32[]{:S(2)}) copy-start(f32[1,320,320]{2,1,0:T(8,128)} %up_ref.1) | copy-start | bytes 1228804
  7.6 1.0 %copy-start.3 = (f32[1,320,320]{2,1,0:T(8,128)S(1)}, f32[1,320,320]{2,1,0:T(8,128)}, u32[]{:S(2)}) copy-start(f32[1,320,320]{2,1,0:T(8,128)} %down_ref.1) | copy-start | bytes 1228804
where the time goes:
time: 65.1 us; the launch traced here: 64.7 us
  Pallas kernels  54.5 us (84%)
  local copies, waits for them, and re-layouts  9.37 us (14%)
  between operations  0.8 us (1%)
    pallas_call x1, Pallas kernels, on_device(): pl.pallas_call(functools.partial(kernel, seq_count, head_count), out_shap...  54.5 us
    unnamed x15, local copies, waits for them, and re-layouts  7.17 us
    pallas_call x1, local copies, waits for them, and re-layouts, on_device(): pl.pallas_call(functools.partial(kernel, seq_count, head_count), out_shap...  1.51 us

commit v1 on v0

--- a/solution.py
+++ b/solution.py
@@ -10,7 +10,6 @@
 
 GROUPS = 2
 NS_ITERS = 4
-LANES = 128
 
 newton_coefs = (3.4445, -4.775, 2.0315)
 MESH = pl.DeviceIdType.MESH
@@ -24,23 +23,30 @@
     )
 
 
-def rms_rows(rows):
-    rows = rows.astype(F32)
-    return (rows * lax.rsqrt(jnp.mean(rows * rows, -1, keepdims=True) + 1e-06)).astype(BF)
+def rms_columns(array):
+    array = array.astype(F32)
+    return (array * lax.rsqrt(jnp.mean(array * array, 0, keepdims=True) + 1e-06)).astype(BF)
 
 
 def kernel(
     seq_count,
     head_count,
+    q_hbm,
+    k_hbm,
+    v_hbm,
+    gate_hbm,
+    up_hbm,
+    down_hbm,
+    step_ref,
+    gain_ref,
+    out_ref,
     q_ref,
     k_ref,
     v_ref,
-    gate_ref,
-    up_ref,
-    down_ref,
-    step_ref,
-    gain_ref,
-    out_ref,
+    first_weights,
+    key_rows,
+    tail_rows,
+    q_own,
     q_all,
     att_own,
     att_all,
@@ -68,12 +74,12 @@
     send_cross,
     send_sq,
     recv_sq,
+    load,
 ):
-    rows, dh = q_ref.shape
+    dh, rows = q_ref.shape
     window = rows // 2
     members = seq_count // GROUPS
     out_rows = rows // seq_count
-    group_rows = rows // GROUPS
     chunk = grad_in.shape[1]
     width = dh * head_count
     me = lax.axis_index("seq")
@@ -104,12 +110,28 @@
             barrier, inc=1, device_id=(me, lax.rem(head + d, head_count)), device_id_type=MESH
         )
 
-    key_t[...] = jnp.transpose(rms_rows(k_ref[...]).astype(F32)).astype(BF)
-    val_t[...] = jnp.transpose(-v_ref[...].astype(F32)).astype(BF)
-    weights[0] = gate_ref[0]
-    weights[1] = up_ref[0]
-    weights[2] = down_ref[0]
-    q_all[me] = q_ref[rows_of(me, out_rows), :]
+    loads = [
+        pltpu.make_async_copy(src, dst, load.at[i])
+        for i, (src, dst) in enumerate(
+            (
+                (k_hbm, k_ref),
+                (v_hbm, v_ref),
+                (gate_hbm.at[0], first_weights.at[0]),
+                (up_hbm.at[0], first_weights.at[1]),
+                (down_hbm.at[0], first_weights.at[2]),
+                (q_hbm, q_ref),
+            )
+        )
+    ]
+    for copy in loads:
+        copy.start()
+    for copy in loads:
+        copy.wait()
+    key_t[...] = rms_columns(k_ref[...])
+    val_t[...] = -v_ref[...]
+    weights[0] = jnp.transpose(first_weights[0])
+    weights[1] = jnp.transpose(first_weights[1])
+    weights[2] = first_weights[2]
     spare = members * chunk - 3 * dh
     if spare:
         grad_f[3 * dh :, :] = jnp.zeros((spare, dh), F32)
@@ -124,7 +146,7 @@
 
     def q_copy(d, slot):
         return remote(
-            q_ref.at[pl.ds(d * out_rows, out_rows), :],
+            q_own.at[d],
             q_all.at[slot],
             send_q.at[d],
             recv_q.at[slot],
@@ -136,7 +158,7 @@
         source = (k_ref, v_ref)[which]
         landing = (tail_k, tail_v)[which]
         return remote(
-            source.at[pl.ds(rows - window, window), :],
+            source.at[:, pl.ds(rows - window, window)],
             landing,
             send_tail.at[which],
             recv_tail.at[which],
@@ -151,37 +173,43 @@
             tail_copy(1, me + 1).start()
 
         for d in range(seq_count):
+            q_own[d] = q_ref[:, d * out_rows : (d + 1) * out_rows]
 
             @pl.when(me != d)
             def _():
                 q_copy(d, me).start()
+
+        q_all[me] = q_own[me]
 
     scale = 1.0 / math.sqrt(dh)
     block = min(256, window)
 
     def attend(start):
-        queries = q_ref[start : start + block, :]
         if start < window:
-            keys = jnp.concatenate([tail_k[start:, :], k_ref[: start + block, :]], 0)
-            values = jnp.concatenate([tail_v[start:, :], v_ref[: start + block, :]], 0)
+            keys = jnp.concatenate([tail_rows[start:, :], key_rows[: start + block, :]], 0)
+            values = jnp.concatenate([tail_v[:, start:], v_ref[:, : start + block]], 1)
         else:
-            keys = k_ref[start - window : start + block, :]
-            values = v_ref[start - window : start + block, :]
-        scores = dot(queries, keys, 1, 1) * scale
-        row = lax.broadcasted_iota(jnp.int32, scores.shape, 0)
-        col = lax.broadcasted_iota(jnp.int32, scores.shape, 1)
-        allowed = (col <= row + window) & (col > row)
+            keys = key_rows[start - window : start + block, :]
+            values = v_ref[:, start - window : start + block]
+        scores = dot(keys, q_ref[:, start : start + block], 1, 0) * scale
+        key = lax.broadcasted_iota(jnp.int32, scores.shape, 0)
+        query = lax.broadcasted_iota(jnp.int32, scores.shape, 1)
+        allowed = (key <= query + window) & (key > query)
         if start < window:
-            allowed = allowed & (col >= jnp.where(me == 0, window - start, 0))
+            allowed = allowed & (key >= jnp.where(me == 0, window - start, 0))
         scores = jnp.where(allowed, scores, -1e30)
-        highest = jnp.max(scores, -1, keepdims=True)
+        highest = jnp.max(scores, 0, keepdims=True)
         expo = jnp.where(allowed, jnp.exp(scores - highest), 0.0)
-        probs = (expo / jnp.sum(expo, -1, keepdims=True)).astype(BF)
-        att_own[start : start + block, :] = dot(probs, values, 1, 0).astype(BF)
+        probs = (expo / jnp.sum(expo, 0, keepdims=True)).astype(BF)
+        mixed = dot(values, probs, 1, 0).astype(BF)
+        piece = min(block, out_rows)
+        for begin in range(0, block, piece):
+            d, low = (start + begin) // out_rows, (start + begin) % out_rows
+            att_own[d, :, low : low + piece] = mixed[:, begin : begin + piece]
 
     def att_copy(d, slot):
         return remote(
-            att_own.at[pl.ds(d * out_rows, out_rows), :],
+            att_own.at[d],
             att_all.at[slot],
             send_att.at[d],
             recv_att.at[slot],
@@ -198,6 +226,10 @@
                 tail_copy(0, me).wait_recv()
                 tail_copy(1, me).wait_recv()
 
+            tail_rows[...] = jnp.transpose(tail_k[...])
+        else:
+            key_rows[...] = jnp.transpose(k_ref[...])
+
         for start in range(begin, begin + window, block):
             attend(start)
         for d in range(begin // out_rows, (begin + window) // out_rows):
@@ -208,9 +240,9 @@
 
             @pl.when(me == d)
             def _():
-                att_all[d] = att_own[d * out_rows : (d + 1) * out_rows, :]
-
-    token_block = min(256, rows)
+                att_all[d] = att_own[d]
+
+    token_block = min(512, rows)
 
     def gradients():
         wb = [weights[i].astype(BF) for i in range(3)]
@@ -218,8 +250,8 @@
         for start in range(0, rows, token_block):
             keys = key_t[:, start : start + token_block]
             values = val_t[:, start : start + token_block]
-            gate = dot(wb[0], keys, 0, 0)
-            upward = dot(wb[1], keys, 0, 0)
+            gate = dot(wb[0], keys, 1, 0)
+            upward = dot(wb[1], keys, 1, 0)
             back = dot(wb[2], values, 1, 0)
             sigma = jax.nn.sigmoid(gate)
             active = gate * sigma
@@ -228,8 +260,8 @@
             grad_gate = (back * upward * slope).astype(BF)
             grad_up = (back * active).astype(BF)
             parts = [
-                dot(keys, grad_gate, 1, 1),
-                dot(keys, grad_up, 1, 1),
+                dot(grad_gate, keys, 1, 1),
+                dot(grad_up, keys, 1, 1),
                 dot(hidden, values, 1, 1),
             ]
             totals = [p if t is None else t + p for t, p in zip(totals, parts)]
@@ -336,18 +368,17 @@
                 q_copy(0, a).wait_recv()
 
         wb = [weights[i].astype(BF) for i in range(3)]
-        normed = rms_rows(
-            q_all[group * members : (group + 1) * members].reshape(group_rows, dh)
-        )
-        gate = dot(normed, wb[0], 1, 0)
-        upward = dot(normed, wb[1], 1, 0)
-        hidden = (gate * jax.nn.sigmoid(gate) * upward).astype(BF)
-        result = dot(hidden, wb[2], 1, 0)
-        fast[group] = result
-        line = dot(jnp.ones((8, dh), BF), (result * result).astype(BF), 1, 1)
-        squares[group, head] = jnp.zeros(squares.shape[2:], F32)
-        for i in range(group_rows // LANES):
-            squares[group, head, i : i + 1, :] = line[0:1, i * LANES : (i + 1) * LANES]
+        down = jnp.transpose(weights[2]).astype(BF)
+        for place, a in enumerate(range(group * members, (group + 1) * members)):
+            normed = rms_columns(q_all[a])
+            gate = dot(wb[0], normed, 1, 0)
+            upward = dot(wb[1], normed, 1, 0)
+            hidden = (gate * jax.nn.sigmoid(gate) * upward).astype(BF)
+            result = dot(down, hidden, 1, 0)
+            fast[a] = result
+            squares[group, head, place : place + 1, :] = jnp.sum(
+                result * result, 0, keepdims=True
+            )
         for h in range(head_count):
 
             @pl.when(head != h)
@@ -370,18 +401,10 @@
         total = squares[group, 0]
         for h in range(1, head_count):
             total = total + squares[group, h]
-        factor = jnp.transpose(lax.rsqrt(total / width + 1e-06))
-        gain = gain_ref[...]
-        piece = min(LANES, out_rows)
-        for start in range(0, group_rows, piece):
-            a, begin = group * members + start // out_rows, start % out_rows
-            lane, low = start // LANES, start % LANES
-            out_ref[a, begin : begin + piece, :] = (
-                att_all[a, begin : begin + piece, :].astype(F32)
-                + gain
-                * fast[group, start : start + piece, :]
-                * factor[low : low + piece, lane : lane + 1]
-            )
+        factor = lax.rsqrt(total / width + 1e-06)
+        gain = jnp.transpose(jnp.broadcast_to(gain_ref[...].reshape(1, dh), (8, dh)))[:, 0:1]
+        for place, a in enumerate(range(group * members, (group + 1) * members)):
+            out_ref[a] = att_all[a].astype(F32) + gain * fast[a] * factor[place : place + 1, :]
 
     for group in range(GROUPS):
 
@@ -463,23 +486,28 @@
         window = rows // 2
         members = seq_count // GROUPS
         out_rows = rows // seq_count
-        group_rows = rows // GROUPS
         chunk = -(-3 * dh // (members * 16)) * 16
-        lines = max(8, group_rows // LANES)
         dma = pltpu.SemaphoreType.DMA
         vmem = pl.BlockSpec(memory_space=pltpu.VMEM)
         smem = pl.BlockSpec(memory_space=pltpu.SMEM)
         return pl.pallas_call(
             functools.partial(kernel, seq_count, head_count),
-            out_shape=jax.ShapeDtypeStruct((seq_count, out_rows, dh), F32),
-            in_specs=[vmem] * 6 + [smem, vmem],
+            out_shape=jax.ShapeDtypeStruct((seq_count, dh, out_rows), F32),
+            in_specs=[pl.BlockSpec(memory_space=pltpu.HBM)] * 6 + [smem, vmem],
             out_specs=vmem,
             scratch_shapes=[
-                pltpu.VMEM((seq_count, out_rows, dh), BF),
+                pltpu.VMEM((dh, rows), BF),
+                pltpu.VMEM((dh, rows), BF),
+                pltpu.VMEM((dh, rows), BF),
+                pltpu.VMEM((3, dh, dh), F32),
                 pltpu.VMEM((rows, dh), BF),
-                pltpu.VMEM((seq_count, out_rows, dh), BF),
                 pltpu.VMEM((window, dh), BF),
-                pltpu.VMEM((window, dh), BF),
+                pltpu.VMEM((seq_count, dh, out_rows), BF),
+                pltpu.VMEM((seq_count, dh, out_rows), BF),
+                pltpu.VMEM((seq_count, dh, out_rows), BF),
+                pltpu.VMEM((seq_count, dh, out_rows), BF),
+                pltpu.VMEM((dh, window), BF),
+                pltpu.VMEM((dh, window), BF),
                 pltpu.VMEM((dh, rows), BF),
                 pltpu.VMEM((dh, rows), BF),
                 pltpu.VMEM((members * chunk, dh), F32),
@@ -487,8 +515,8 @@
                 pltpu.VMEM((members, chunk, dh), BF),
                 pltpu.VMEM((GROUPS, members * chunk, dh), BF),
                 pltpu.VMEM((3, dh, dh), F32),
-                pltpu.VMEM((GROUPS, group_rows, dh), F32),
-                pltpu.VMEM((GROUPS, head_count, lines, LANES), F32),
+                pltpu.VMEM((seq_count, dh, out_rows), F32),
+                pltpu.VMEM((GROUPS, head_count, members, out_rows), F32),
                 dma((seq_count,)),
                 dma((seq_count,)),
                 dma((seq_count,)),
@@ -502,20 +530,21 @@
                 dma((GROUPS,)),
                 dma((GROUPS, head_count)),
                 dma((GROUPS, head_count)),
+                dma((6,)),
             ],
             compiler_params=pltpu.CompilerParams(
-                collective_id=0, has_side_effects=True, vmem_limit_bytes=48 * 1024 * 1024
+                collective_id=0, has_side_effects=True, vmem_limit_bytes=60 * 1024 * 1024
             ),
         )(
-            queries,
-            key_vectors,
-            value_vectors,
+            queries.T,
+            key_vectors.T,
+            value_vectors.T,
             fast_gate,
             fast_up,
             fast_down,
             step_sizes,
-            out_gain.reshape(1, dh),
-        )
+            out_gain,
+        ).swapaxes(1, 2)
 
     in_specs = (
         P("seq", "head"),

time: 65.1 us -> 59.2 us (0.909)
  local copies, waits for them, and re-layouts: 9.37 us -> 2.46 us
  Pallas kernels: 54.5 us -> 55.9 us
    unnamed x15 -> x1, local copies, waits for them, and re-layouts: 7.17 us -> 2.46 us
    pallas_call x1 -> x0, local copies, waits for them, and re-layouts: 1.51 us -> none  [on_device(): pl.pallas_call(functools.partial(kernel, seq_count, head_count), out_shap...]
    pallas_call x1, Pallas kernels: 54.5 us -> 55.9 us  [on_device(): pl.pallas_call(functools.partial(kernel, seq_count, head_count), out_shap...]
    reshape x1 -> x0, local copies, waits for them, and re-layouts: 0.68 us -> none  [on_device(): out_gain.reshape(1, dh)]
where the time goes in v1:
time: 59.2 us; the launch traced here: 59 us
  Pallas kernels  55.9 us (94%)
  local copies, waits for them, and re-layouts  2.46 us (4%)
  between operations  0.66 us (1%)
    pallas_call x1, Pallas kernels, on_device(): pl.pallas_call(functools.partial(kernel, seq_count, head_count), out_shap...  55.9 us
    unnamed x1, local copies, waits for them, and re-layouts  2.46 us

profile of v1, /device:TPU:1, one launch (start us, length us, event | category | flops | bytes accessed | tf_op | source)
XLA Modules:
  0.0 59.0 jit_solution(16441198013671224785)
XLA Ops:
  0.7 55.9 %shard_map.82 = f32[4,320,256]{2,1,0:T(8,128)} custom-call(bf16[320,1024]{1,0:T(8,128)(2,1)} %bitcast.5, bf16[320,1024]{1,0:T(8,128)(2,1)} %bitcast.6, bf16[320,1024]{1,0:T(8,128)(2,1)} %bitcast.7, f32[1,320,320]{2,1,0:T(8,128)} %gate_hbm.1, f32[1,320,320]{2,1,0:T(8,128)} %up_hbm.1, f32[1,320,320]{2,1,0:T(8,128)} %down_hbm.1, f32[1]{0:T(128)S(6)} %copy.10.step_ref, ...), custom_call_target="tpu_custom_call" | custom-call | tf_op jit(solution)/shard_map/pallas_call | solution.py:493
  56.5 2.5 %copy.11 = f32[4,256,320]{1,2,0:T(8,128)} copy(f32[4,256,320]{1,2,0:T(8,128)} %bitcast.4) | data formatting | bytes 2621440

commit v2 on v1

--- a/solution.py
+++ b/solution.py
@@ -80,7 +80,8 @@
     window = rows // 2
     members = seq_count // GROUPS
     out_rows = rows // seq_count
-    chunk = grad_in.shape[1]
+    chunk = grad_in.shape[2]
+    matrix_rows = members * chunk
     width = dh * head_count
     me = lax.axis_index("seq")
     head = lax.axis_index("head")
@@ -132,10 +133,11 @@
     weights[0] = jnp.transpose(first_weights[0])
     weights[1] = jnp.transpose(first_weights[1])
     weights[2] = first_weights[2]
-    spare = members * chunk - 3 * dh
+    spare = matrix_rows - dh
     if spare:
-        grad_f[3 * dh :, :] = jnp.zeros((spare, dh), F32)
-        grad_b[3 * dh :, :] = jnp.zeros((spare, dh), BF)
+        for i in range(3):
+            grad_f[i, dh:, :] = jnp.zeros((spare, dh), F32)
+            grad_b[i, dh:, :] = jnp.zeros((spare, dh), BF)
 
     @pl.when(me == 0)
     def _():
@@ -266,76 +268,86 @@
             ]
             totals = [p if t is None else t + p for t, p in zip(totals, parts)]
         for i in range(3):
-            grad_f[i * dh : (i + 1) * dh, :] = totals[i]
-            grad_b[i * dh : (i + 1) * dh, :] = totals[i].astype(BF)
-
-    def part_copy(group, target, slot):
+            grad_f[i, :dh, :] = totals[i]
+            grad_b[i, :dh, :] = totals[i].astype(BF)
+
+    def part_copy(group, i, target, slot):
         return remote(
-            grad_b.at[pl.ds(target * chunk, chunk), :],
-            grad_in.at[slot],
-            send_part.at[target],
-            recv_part.at[slot],
+            grad_b.at[i, pl.ds(target * chunk, chunk), :],
+            grad_in.at[i, slot],
+            send_part.at[i, target],
+            recv_part.at[i, slot],
             group * members + target,
             head,
         )
 
-    def sum_copy(group, piece, send, seq):
-        place = sums.at[group, rows_of(piece, chunk), :]
-        return remote(place, place, send, recv_sum.at[group, piece], seq, head)
-
-    def spread(group):
+    def sum_copy(group, i, piece, send, seq):
+        place = sums.at[group, i, rows_of(piece, chunk), :]
+        return remote(place, place, send, recv_sum.at[group, i, piece], seq, head)
+
+    def spread(group, i):
         for m in range(members):
 
             @pl.when(own_member != m)
             def _():
                 sum_copy(
-                    group, own_member, send_sum.at[group, m], own_group * members + m
+                    group, i, own_member, send_sum.at[group, i, m], own_group * members + m
                 ).start()
 
     def group_sums(group):
         gradients()
-        for m in range(members):
-
-            @pl.when(own_member != m)
-            def _():
-                part_copy(group, m, own_member).start()
+        for i in range(3):
+            for m in range(members):
+
+                @pl.when(own_member != m)
+                def _():
+                    part_copy(group, i, m, own_member).start()
+
+            grad_in[i, own_member] = jnp.zeros(grad_in.shape[2:], BF)
 
         place = rows_of(own_member, chunk)
-        grad_in[own_member] = jnp.zeros(grad_in.shape[1:], BF)
-        for m in range(members):
-
-            @pl.when(own_member != m)
-            def _():
-                part_copy(group, m, m).wait_recv()
-
-        total = grad_f[place, :]
-        for m in range(members):
-            total = total + grad_in[m].astype(F32)
-        sums[group, place, :] = total.astype(BF)
-        for other in range(GROUPS):
-            if other != group:
-                sum_copy(
-                    group, own_member, send_cross.at[other], other * members + own_member
-                ).start()
-        spread(group)
-
-    def collect_sums(group):
-        @pl.when(own_group != group)
-        def _():
-            sum_copy(group, own_member, send_cross.at[group], me).wait_recv()
-            spread(group)
-
-        for m in range(members):
-
-            @pl.when(own_member != m)
-            def _():
-                sum_copy(group, m, send_cross.at[group], me).wait_recv()
-
-    def update(group):
+        for i in range(3):
+            for m in range(members):
+
+                @pl.when(own_member != m)
+                def _():
+                    part_copy(group, i, m, m).wait_recv()
+
+            total = grad_f[i, place, :]
+            for m in range(members):
+                total = total + grad_in[i, m].astype(F32)
+            sums[group, i, place, :] = total.astype(BF)
+            for other in range(GROUPS):
+                if other != group:
+                    sum_copy(
+                        group,
+                        i,
+                        own_member,
+                        send_cross.at[other, i],
+                        other * members + own_member,
+                    ).start()
+            spread(group, i)
+
+    def collect_sums(group, matrices):
+        for i in matrices:
+
+            @pl.when(own_group != group)
+            def _():
+                sum_copy(group, i, own_member, send_cross.at[group, i], me).wait_recv()
+                spread(group, i)
+
+        for i in matrices:
+            for m in range(members):
+
+                @pl.when(own_member != m)
+                def _():
+                    sum_copy(group, i, m, send_cross.at[group, i], me).wait_recv()
+
+    def update(group, matrices):
         first, second, third = newton_coefs
         current = []
-        for i in range(3):
-            grads = sums[group, i * dh : (i + 1) * dh, :].astype(F32)
+        for i in matrices:
+            grads = sums[group, i, :dh, :].astype(F32)
             total = jnp.sum(jnp.sum(grads * grads, 1, keepdims=True), 0, keepdims=True)
             current.append(grads * lax.rsqrt(total + 1e-06))
         for repeat in range(NS_ITERS):
@@ -347,8 +359,8 @@
             current = [
                 first * x + dot(b, y, 1, 0) for x, b, y in zip(current, mixing, low)
             ]
-        for i in range(3):
-            weights[i] = weights[i] - step_ref[0] * current[i]
+        for i, x in zip(matrices, current):
+            weights[i] = weights[i] - step_ref[0] * x
 
     def sq_copy(group, target, slot):
         return remote(
@@ -432,8 +444,9 @@
                     attend_half(True)
 
             apply_group(group - 1)
-        collect_sums(group)
-        update(group)
+        for matrices in ((0,), (1, 2)):
+            collect_sums(group, matrices)
+            update(group, matrices)
     apply_group(GROUPS - 1)
     for group in range(GROUPS):
         finish_group(group)
@@ -450,23 +463,28 @@
             q_copy(d, me).wait_send()
             att_copy(d, me).wait_send()
 
-    for m in range(members):
-
-        @pl.when(own_member != m)
-        def _():
-            part_copy(own_group, m, own_member).wait_send()
-            for group in range(GROUPS):
+    for i in range(3):
+        for m in range(members):
+
+            @pl.when(own_member != m)
+            def _():
+                part_copy(own_group, i, m, own_member).wait_send()
+                for group in range(GROUPS):
+                    sum_copy(
+                        group, i, own_member, send_sum.at[group, i, m], own_group * members + m
+                    ).wait_send()
+
+        for other in range(GROUPS):
+
+            @pl.when(own_group != other)
+            def _():
                 sum_copy(
-                    group, own_member, send_sum.at[group, m], own_group * members + m
+                    own_group,
+                    i,
+                    own_member,
+                    send_cross.at[other, i],
+                    other * members + own_member,
                 ).wait_send()
-
-    for other in range(GROUPS):
-
-        @pl.when(own_group != other)
-        def _():
-            sum_copy(
-                own_group, own_member, send_cross.at[other], other * members + own_member
-            ).wait_send()
 
     for group in range(GROUPS):
         for h in range(head_count):
@@ -486,7 +504,7 @@
         window = rows // 2
         members = seq_count // GROUPS
         out_rows = rows // seq_count
-        chunk = -(-3 * dh // (members * 16)) * 16
+        chunk = -(-dh // (members * 16)) * 16
         dma = pltpu.SemaphoreType.DMA
         vmem = pl.BlockSpec(memory_space=pltpu.VMEM)
         smem = pl.BlockSpec(memory_space=pltpu.SMEM)
@@ -510,10 +528,10 @@
                 pltpu.VMEM((dh, window), BF),
                 pltpu.VMEM((dh, rows), BF),
                 pltpu.VMEM((dh, rows), BF),
-                pltpu.VMEM((members * chunk, dh), F32),
-                pltpu.VMEM((members * chunk, dh), BF),
-                pltpu.VMEM((members, chunk, dh), BF),
-                pltpu.VMEM((GROUPS, members * chunk, dh), BF),
+                pltpu.VMEM((3, members * chunk, dh), F32),
+                pltpu.VMEM((3, members * chunk, dh), BF),
+                pltpu.VMEM((3, members, chunk, dh), BF),
+                pltpu.VMEM((GROUPS, 3, members * chunk, dh), BF),
                 pltpu.VMEM((3, dh, dh), F32),
                 pltpu.VMEM((seq_count, dh, out_rows), F32),
                 pltpu.VMEM((GROUPS, head_count, members, out_rows), F32),
@@ -523,11 +541,11 @@
                 dma((seq_count,)),
                 dma((2,)),
                 dma((2,)),
-                dma((members,)),
-                dma((members,)),
-                dma((GROUPS, members)),
-                dma((GROUPS, members)),
-                dma((GROUPS,)),
+                dma((3, members)),
+                dma((3, members)),
+                dma((GROUPS, 3, members)),
+                dma((GROUPS, 3, members)),
+                dma((GROUPS, 3)),
                 dma((GROUPS, head_count)),
                 dma((GROUPS, head_count)),
                 dma((6,)),

time: 59.2 us -> 54.6 us (0.922)
  Pallas kernels: 55.9 us -> 51 us
    pallas_call x1, Pallas kernels: 55.9 us -> 51 us  [on_device(): pl.pallas_call(functools.partial(kernel, seq_count, head_count), out_shap...]
where the time goes in v2:
time: 54.6 us; the launch traced here: 54.1 us
  Pallas kernels  51 us (93%)
  local copies, waits for them, and re-layouts  2.46 us (5%)
  between operations  0.66 us (1%)
    pallas_call x1, Pallas kernels, on_device(): pl.pallas_call(functools.partial(kernel, seq_count, head_count), out_shap...  51 us
    unnamed x1, local copies, waits for them, and re-layouts  2.46 us

profile of v2, /device:TPU:1, one launch (start us, length us, event | category | flops | bytes accessed | tf_op | source)
XLA Modules:
  0.0 54.1 jit_solution(6500826211822302678)
XLA Ops:
  0.7 51.0 %shard_map.82 = f32[4,320,256]{2,1,0:T(8,128)} custom-call(bf16[320,1024]{1,0:T(8,128)(2,1)} %bitcast.5, bf16[320,1024]{1,0:T(8,128)(2,1)} %bitcast.6, bf16[320,1024]{1,0:T(8,128)(2,1)} %bitcast.7, f32[1,320,320]{2,1,0:T(8,128)} %gate_hbm.1, f32[1,320,320]{2,1,0:T(8,128)} %up_hbm.1, f32[1,320,320]{2,1,0:T(8,128)} %down_hbm.1, f32[1]{0:T(128)S(6)} %copy.10.step_ref, ...), custom_call_target="tpu_custom_call" | custom-call | tf_op jit(solution)/shard_map/pallas_call | solution.py:511
  51.7 2.5 %copy.11 = f32[4,256,320]{1,2,0:T(8,128)} copy(f32[4,256,320]{1,2,0:T(8,128)} %bitcast.4) | data formatting | bytes 2621440
